TPU v7x, 32 devices: a whole 2x2x4 slice. The times are simulated.
32 devices in a mesh: dp: 32 (over z, y, x, core).
Axes of the slice: x: 2, y: 2, z: 4, core: 2. Of those that a mesh axis runs over, the one named last changes fastest.
Arguments:
- grads: bfloat16 [32, 512, 128], P('dp'), may hold values from -3200 to 3200
- master: float32 [512, 128], P('dp'), may hold values from -6 to 6
- first_q: bfloat16 [512, 128], P('dp'), may hold values from -1 to 1
- first_scale: float32 [512], P('dp'), may hold values from 0.005 to 0.05
- second_q: bfloat16 [512, 128], P('dp'), may hold values from 0.099609375 to 1
- second_scale: float32 [512], P('dp'), may hold values from 2e-05 to 0.0002
Outputs:
- weights: bfloat16 [512, 128], replicated
- master_new: float32 [512, 128], P('dp')
- first_q_new: bfloat16 [512, 128], P('dp')
- first_scale_new: float32 [512], P('dp')
- second_q_new: bfloat16 [512, 128], P('dp')
- second_scale_new: float32 [512], P('dp')
All inputs are finite; a program needn't handle non-finite values. Where the computation divides by a largest or mean magnitude, that divisor is 1e-20 or more.
Results may differ from a plain program's by a relative error of at most 0.001.
Values may be sent and summed in bfloat16 or wider, within the bound.
A program may use at most 64 MiB of HBM per device.

v0:
```python
import jax
import jax.numpy as jnp
from jax import lax
from jax.sharding import PartitionSpec as P

beta_one = 0.9
beta_two = 0.95
learn_rate = 0.05
decay_rate = 0.1
adam_epsilon = 1e-08
clip_rms = 0.01
first_fix = 1.0 - 0.9**10
second_fix = 1.0 - 0.95**10


def from_partner(block, axis, stride):
    count = lax.axis_size(axis)
    route = []
    for low in range(count):
        high = low | 1 << stride
        if high != low and high < count:
            route += [(low, high), (high, low)]
    return lax.ppermute(block, axis, route)


def advance(clipped, master, first_q, first_scale, second_q, second_scale):
    first = first_q.astype(jnp.float32) * first_scale[:, None]
    second = second_q.astype(jnp.float32) * second_scale[:, None]
    first_new = beta_one * first + (1.0 - beta_one) * clipped
    second_new = beta_two * second + (1.0 - beta_two) * clipped * clipped
    change = first_new / first_fix / (jnp.sqrt(second_new / second_fix) + adam_epsilon)
    master_new = master * (1.0 - learn_rate * decay_rate) - learn_rate * change
    first_scale_new = jnp.max(jnp.abs(first_new), axis=1) + 1e-08
    second_scale_new = jnp.max(jnp.abs(second_new), axis=1) + 1e-08
    first_q_new = (first_new / first_scale_new[:, None]).astype(jnp.bfloat16)
    second_q_new = (second_new / second_scale_new[:, None]).astype(jnp.bfloat16)
    return (master_new, first_q_new, first_scale_new, second_q_new, second_scale_new)


def split_half(current, index, bit):
    half = current.shape[0] // 2
    upper = index >> bit & 1
    keeping = lax.dynamic_slice_in_dim(current, upper * half, half, 0)
    sending = lax.dynamic_slice_in_dim(current, (1 - upper) * half, half, 0)
    return (keeping, sending)


def shards(grads, master, first_q, first_scale, second_q, second_scale):
    local = grads[0]
    index = lax.axis_index("dp")
    levels = lax.axis_size("dp").bit_length() - 1
    keeping, sending = split_half(local, index, levels - 1)
    arrived = from_partner(sending, "dp", levels - 1)
    total = keeping.astype(jnp.float32) + arrived.astype(jnp.float32)
    for level in range(levels - 2, -1, -1):
        keeping, sending = split_half(total, index, level)
        arrived = from_partner(sending, "dp", level)
        total = keeping + arrived
    squares = lax.psum(jnp.sum(total * total), "dp")
    limit = clip_rms * jnp.sqrt(jnp.float32(local.shape[0] * local.shape[1]))
    factor = jnp.minimum(1.0, limit / (jnp.sqrt(squares) + 1e-06))
    clipped = factor * total
    master_new, first_q_new, first_scale_new, second_q_new, second_scale_new = advance(
        clipped, master, first_q, first_scale, second_q, second_scale
    )
    weights = lax.all_gather(master_new.astype(jnp.bfloat16), "dp", axis=0, tiled=True)
    return (weights, master_new, first_q_new, first_scale_new, second_q_new, second_scale_new)


def solution(mesh):
    placed = (P("dp", None, None), P("dp", None), P("dp", None), P("dp"), P("dp", None), P("dp"))
    return jax.shard_map(
        shards,
        mesh=mesh,
        in_specs=placed,
        out_specs=(P(), P("dp", None), P("dp", None), P("dp"), P("dp", None), P("dp")),
        check_vma=False,
    )
```

profile of v0, /device:TPU:0, one launch (start us, length us, event | category | flops | bytes accessed | tf_op | source)
XLA Modules:
  0.0 108.1 jit_solution(11565756240725620342)
XLA Ops:
  0.6 0.9 dynamic-slice_bitcast_fusion
  1.6 4.0 %collective-permute-start = (bf16[256,128]{1,0:T(8,128)(2,1)S(1)}, bf16[256,128]{1,0:T(8,128)(2,1)S(1)}, u32[]{:S(2)}, u32[]{:S(2)}) collective-permute-start(bf16[256,128]{1,0:T(8,128)(2,1)S(1)} %dynamic-slice_bitcast_fusion), channel_id=1, source_target_pairs={{0,16},{16,0},{1,17},{17,1},{2,18},{18,2},{3,19},{19,3},{4,20},{20... | collective-permute-start | bytes 196616 | tf_op jit(solution)/shard_map/ppermute | solution.py:23
  5.6 3.6 %collective-permute-done = bf16[256,128]{1,0:T(8,128)(2,1)S(1)} collective-permute-done((bf16[256,128]{1,0:T(8,128)(2,1)S(1)}, bf16[256,128]{1,0:T(8,128)(2,1)S(1)}, u32[]{:S(2)}, u32[]{:S(2)}) %collective-permute-start) | collective-permute-done | bytes 65568 | tf_op jit(solution)/shard_map/ppermute | solution.py:23
  9.3 0.6 collective-permute-start.1
  9.9 3.7 %collective-permute-done.1 = f32[128,128]{1,0:T(8,128)S(1)} collective-permute-done((f32[128,128]{1,0:T(8,128)S(1)}, f32[128,128]{1,0:T(8,128)S(1)}, u32[]{:S(2)}, u32[]{:S(2)}) %collective-permute-start.1) | collective-permute-done | bytes 65568 | tf_op jit(solution)/shard_map/ppermute | solution.py:23
  13.6 1.8 %collective-permute-start.2 = (f32[64,128]{1,0:T(8,128)S(1)}, f32[64,128]{1,0:T(8,128)S(1)}, u32[]{:S(2)}, u32[]{:S(2)}) collective-permute-start(f32[64,128]{1,0:T(8,128)S(1)} %constant_dynamic-slice_fusion.2), channel_id=1, source_target_pairs={{0,4},{4,0},{1,5},{5,1},{2,6},{6,2},{3,7},{7,3},{8,12},{12,8},{9,1... | collective-permute-start | bytes 98312 | tf_op jit(solution)/shard_map/ppermute | solution.py:23
  15.4 2.2 %collective-permute-done.2 = f32[64,128]{1,0:T(8,128)S(1)} collective-permute-done((f32[64,128]{1,0:T(8,128)S(1)}, f32[64,128]{1,0:T(8,128)S(1)}, u32[]{:S(2)}, u32[]{:S(2)}) %collective-permute-start.2) | collective-permute-done | bytes 32800 | tf_op jit(solution)/shard_map/ppermute | solution.py:23
  17.6 1.8 %collective-permute-start.3 = (f32[32,128]{1,0:T(8,128)S(1)}, f32[32,128]{1,0:T(8,128)S(1)}, u32[]{:S(2)}, u32[]{:S(2)}) collective-permute-start(f32[32,128]{1,0:T(8,128)S(1)} %constant_dynamic-slice_fusion.1), channel_id=1, source_target_pairs={{0,2},{2,0},{1,3},{3,1},{4,6},{6,4},{5,7},{7,5},{8,10},{10,8},{9,1... | collective-permute-start | bytes 49160 | tf_op jit(solution)/shard_map/ppermute | solution.py:23
  19.4 2.0 %collective-permute-done.3 = f32[32,128]{1,0:T(8,128)S(1)} collective-permute-done((f32[32,128]{1,0:T(8,128)S(1)}, f32[32,128]{1,0:T(8,128)S(1)}, u32[]{:S(2)}, u32[]{:S(2)}) %collective-permute-start.3) | collective-permute-done | bytes 16416 | tf_op jit(solution)/shard_map/ppermute | solution.py:23
  21.5 1.2 %collective-permute-done.4 = f32[16,128]{1,0:T(8,128)S(1)} collective-permute-done((f32[16,128]{1,0:T(8,128)S(1)}, f32[16,128]{1,0:T(8,128)S(1)}, u32[]{:S(2)}, u32[]{:S(2)}) %collective-permute-start.4) | collective-permute-done | bytes 8224 | tf_op jit(solution)/shard_map/ppermute | solution.py:23
  22.6 0.6 multiply_reduce_fusion
  23.2 40.0 %psum.7 = f32[]{:T(128)} all-reduce(f32[]{:T(128)} %get-tuple-element.10), channel_id=1, replica_groups=mesh['dp'=32] {'dp'}, use_global_device_ids=true, to_apply=%region_1.0 | all-reduce | flops 1 | bytes 8 | tf_op jit(solution)/shard_map/psum | solution.py:59
  63.9 0.0 copy-start.1
  64.0 0.0 copy-start.4
  64.0 0.0 copy-start.5
  64.0 0.6 copy-done.1
  64.6 0.0 copy-done.4
  64.6 0.0 copy-done.5
  64.7 0.8 abs_reduce_fusion
  65.5 40.8 %all_gather.3 = bf16[512,128]{1,0:T(8,128)(2,1)S(1)} all-gather(bf16[16,128]{1,0:T(8,128)(2,1)S(1)} %get-tuple-element.12), channel_id=1, replica_groups=mesh['dp'=32] {'dp'}, dimensions={0}, use_global_device_ids=true | all-gather | bytes 135168 | tf_op jit(solution)/shard_map/all_gather | solution.py:66
  106.3 0.5 copy-done.6
  106.8 0.0 copy-done.7
  106.8 0.7 divide_convert_fusion
  107.5 0.7 copy.13
  (18 shorter events, 0.1 us)
Async XLA Ops:
  0.6 8.6 %copy-start = (bf16[1,512,128]{2,1,0:T(8,128)(2,1)S(1)}, bf16[1,512,128]{2,1,0:T(8,128)(2,1)}, u32[]{:S(2)}) copy-start(bf16[1,512,128]{2,1,0:T(8,128)(2,1)} %param.6) | copy-start | bytes 393220
  1.6 7.7 %collective-permute-start = (bf16[256,128]{1,0:T(8,128)(2,1)S(1)}, bf16[256,128]{1,0:T(8,128)(2,1)S(1)}, u32[]{:S(2)}, u32[]{:S(2)}) collective-permute-start(bf16[256,128]{1,0:T(8,128)(2,1)S(1)} %dynamic-slice_bitcast_fusion), channel_id=1, source_target_pairs={{0,16},{16,0},{1,17},{17,1},{2,18},{18,2},{3,19},{19,3},{4,20},{20... | collective-permute-start | bytes 196616 | tf_op jit(solution)/shard_map/ppermute | solution.py:23
  9.3 4.3 %collective-permute-start.1 = (f32[128,128]{1,0:T(8,128)S(1)}, f32[128,128]{1,0:T(8,128)S(1)}, u32[]{:S(2)}, u32[]{:S(2)}) collective-permute-start(f32[128,128]{1,0:T(8,128)S(1)} %constant_dynamic-slice_fusion.3), channel_id=1, source_target_pairs={{0,8},{8,0},{1,9},{9,1},{2,10},{10,2},{3,11},{11,3},{4,12},{12,4},... | collective-permute-start | bytes 196616 | tf_op jit(solution)/shard_map/ppermute | solution.py:23
  13.6 4.0 %collective-permute-start.2 = (f32[64,128]{1,0:T(8,128)S(1)}, f32[64,128]{1,0:T(8,128)S(1)}, u32[]{:S(2)}, u32[]{:S(2)}) collective-permute-start(f32[64,128]{1,0:T(8,128)S(1)} %constant_dynamic-slice_fusion.2), channel_id=1, source_target_pairs={{0,4},{4,0},{1,5},{5,1},{2,6},{6,2},{3,7},{7,3},{8,12},{12,8},{9,1... | collective-permute-start | bytes 98312 | tf_op jit(solution)/shard_map/ppermute | solution.py:23
  17.6 3.8 %collective-permute-start.3 = (f32[32,128]{1,0:T(8,128)S(1)}, f32[32,128]{1,0:T(8,128)S(1)}, u32[]{:S(2)}, u32[]{:S(2)}) collective-permute-start(f32[32,128]{1,0:T(8,128)S(1)} %constant_dynamic-slice_fusion.1), channel_id=1, source_target_pairs={{0,2},{2,0},{1,3},{3,1},{4,6},{6,4},{5,7},{7,5},{8,10},{10,8},{9,1... | collective-permute-start | bytes 49160 | tf_op jit(solution)/shard_map/ppermute | solution.py:23
  21.5 1.2 %collective-permute-start.4 = (f32[16,128]{1,0:T(8,128)S(1)}, f32[16,128]{1,0:T(8,128)S(1)}, u32[]{:S(2)}, u32[]{:S(2)}) collective-permute-start(f32[16,128]{1,0:T(8,128)S(1)} %constant_dynamic-slice_fusion), channel_id=1, source_target_pairs={{0,1},{1,0},{2,3},{3,2},{4,5},{5,4},{6,7},{7,6},{8,9},{9,8},{10,11... | collective-permute-start | bytes 24584 | tf_op jit(solution)/shard_map/ppermute | solution.py:23
  22.6 41.4 %copy-start.3 = (f32[16,128]{1,0:T(8,128)S(1)}, f32[16,128]{1,0:T(8,128)}, u32[]{:S(2)}) copy-start(f32[16,128]{1,0:T(8,128)} %param.7) | copy-start | bytes 24580
  63.2 0.8 copy-start.2
  63.9 0.7 copy-start.1
  64.0 0.7 copy-start.4
  64.0 0.7 copy-start.5
  106.3 0.5 copy-start.6
  106.3 0.5 copy-start.7
where the time goes:
time: 109 us; the launch traced here: 108 us
  blocking collectives  80.8 us (74%)
  waiting for transfers between devices  12.7 us (12%)
  starting transfers between devices  8.24 us (8%)
  local copies, waits for them, and re-layouts  2.76 us (3%)
  other arithmetic  2.12 us (2%)
  between operations  1.48 us (1%)
    all_gather x1, blocking collectives, shards(): lax.all_gather(master_new.astype(jnp.bfloat16), 'dp', axis=0, tiled=True)  40.8 us
    psum x1, blocking collectives, shards(): squares = lax.psum(jnp.sum(total * total), 'dp')  40 us
    ppermute x5, waiting for transfers between devices, from_partner(): return lax.ppermute(block, axis, route)  12.7 us
    ppermute x5, starting transfers between devices, from_partner(): return lax.ppermute(block, axis, route)  8.24 us
  transfers between devices with their start and end apart: 5, of which 5 were waited for; matrix products, arithmetic and copies ran while one was open for 0% of the time, Pallas kernels for 0%

commit v1 on v0

v1 whole, which is shorter than its diff:
```python
import functools

import jax
import jax.numpy as jnp
from jax import lax
from jax.experimental import pallas as pl
from jax.experimental.pallas import tpu as pltpu
from jax.sharding import PartitionSpec as P

MESH = pl.DeviceIdType.MESH

beta_one = 0.9
beta_two = 0.95
learn_rate = 0.05
decay_rate = 0.1
adam_epsilon = 1e-08
clip_rms = 0.01
first_fix = 1.0 - 0.9**10
second_fix = 1.0 - 0.95**10


def column_of(row, count):
    down = lax.broadcasted_iota(jnp.int32, (count, count), 0)
    along = lax.broadcasted_iota(jnp.int32, (count, count), 1)
    spread = jnp.broadcast_to(row, (count, count))
    return jnp.sum(jnp.where(down == along, spread, 0.0), axis=1, keepdims=True)


def row_of(column, count):
    down = lax.broadcasted_iota(jnp.int32, (count, count), 0)
    along = lax.broadcasted_iota(jnp.int32, (count, count), 1)
    spread = jnp.broadcast_to(column, (count, count))
    return jnp.sum(jnp.where(down == along, spread, 0.0), axis=0, keepdims=True)


def step_kernel(
    n,
    entries,
    grads_ref,
    master_ref,
    first_q_ref,
    first_scale_ref,
    second_q_ref,
    second_scale_ref,
    weights_ref,
    master_new_ref,
    first_q_new_ref,
    first_scale_new_ref,
    second_q_new_ref,
    second_scale_new_ref,
    local,
    arrived,
    squares,
    mine,
    stage_sem,
    keep_sem,
    grad_send,
    grad_recv,
    norm_send,
    norm_recv,
    gather_send,
    gather_recv,
):
    me = lax.axis_index("dp")
    own = master_ref.shape[0]
    width = master_ref.shape[1]

    stage = pltpu.make_async_copy(grads_ref.at[0], local, stage_sem)
    stage.start()

    barrier = pltpu.get_barrier_semaphore()

    def greet(k, carry):
        pl.semaphore_signal(barrier, inc=1, device_id=(lax.rem(me + k, n),), device_id_type=MESH)
        return carry

    lax.fori_loop(1, n, greet, 0)
    stage.wait()
    pl.semaphore_wait(barrier, n - 1)

    def send_grad(k, carry):
        to = lax.rem(me + k, n)
        pltpu.make_async_remote_copy(
            src_ref=local.at[pl.ds(pl.multiple_of(to * own, own), own)],
            dst_ref=arrived.at[k - 1],
            send_sem=grad_send,
            recv_sem=grad_recv,
            device_id=(to,),
            device_id_type=MESH,
        ).start()
        return carry

    lax.fori_loop(1, n, send_grad, 0)

    total = local[pl.ds(pl.multiple_of(me * own, own), own), :].astype(jnp.float32)
    pltpu.make_async_copy(arrived, arrived, grad_recv).wait()
    total = total + jnp.sum(arrived[...].astype(jnp.float32), axis=0)

    squares[pl.ds(n - 1, 1), :] = jnp.sum(total * total, axis=0, keepdims=True)

    def send_norm(k, carry):
        pltpu.make_async_remote_copy(
            src_ref=squares.at[pl.ds(n - 1, 1)],
            dst_ref=squares.at[pl.ds(k - 1, 1)],
            send_sem=norm_send,
            recv_sem=norm_recv,
            device_id=(lax.rem(me + k, n),),
            device_id_type=MESH,
        ).start()
        return carry

    lax.fori_loop(1, n, send_norm, 0)

    first = first_q_ref[...].astype(jnp.float32) * column_of(first_scale_ref[...], own)
    second = second_q_ref[...].astype(jnp.float32) * column_of(second_scale_ref[...], own)
    kept = master_ref[...] * (1.0 - learn_rate * decay_rate)
    others = squares.at[pl.ds(0, n - 1)]
    pltpu.make_async_copy(others, others, norm_recv).wait()
    norm = jnp.sqrt(jnp.sum(squares[...], keepdims=True))
    limit = clip_rms * jnp.sqrt(jnp.float32(entries))
    factor = jnp.minimum(1.0, limit / (norm + 1e-06))
    clipped = factor * total
    first_new = beta_one * first + (1.0 - beta_one) * clipped
    second_new = beta_two * second + (1.0 - beta_two) * clipped * clipped
    change = first_new / first_fix / (jnp.sqrt(second_new / second_fix) + adam_epsilon)
    master_new = kept - learn_rate * change
    mine[...] = master_new.astype(jnp.bfloat16)

    slot = weights_ref.at[pl.ds(pl.multiple_of(me * own, own), own)]

    def send_weights(k, carry):
        pltpu.make_async_remote_copy(
            src_ref=mine,
            dst_ref=slot,
            send_sem=gather_send,
            recv_sem=gather_recv,
            device_id=(lax.rem(me + k, n),),
            device_id_type=MESH,
        ).start()
        return carry

    lax.fori_loop(1, n, send_weights, 0)
    keep = pltpu.make_async_copy(mine, slot, keep_sem)
    keep.start()

    master_new_ref[...] = master_new
    first_top = jnp.max(jnp.abs(first_new), axis=1, keepdims=True) + 1e-08
    second_top = jnp.max(jnp.abs(second_new), axis=1, keepdims=True) + 1e-08
    first_q_new_ref[...] = (first_new / first_top).astype(jnp.bfloat16)
    second_q_new_ref[...] = (second_new / second_top).astype(jnp.bfloat16)
    first_scale_new_ref[...] = row_of(first_top, own)
    second_scale_new_ref[...] = row_of(second_top, own)

    keep.wait()
    sent = local.at[pl.ds(0, (n - 1) * own)]
    gathered = weights_ref.at[pl.ds(0, (n - 1) * own)]
    pltpu.make_async_copy(sent, sent, grad_send).wait()
    pltpu.make_async_copy(others, others, norm_send).wait()
    pltpu.make_async_copy(sent, sent, gather_send).wait()
    pltpu.make_async_copy(gathered, gathered, gather_recv).wait()


def shards(grads, master, first_q, first_scale, second_q, second_scale):
    n = lax.axis_size("dp")
    blocks, width = grads.shape[1:]
    own = master.shape[0]
    vmem = pl.BlockSpec(memory_space=pltpu.VMEM)
    hbm = pl.BlockSpec(memory_space=pl.ANY)
    shape = jax.ShapeDtypeStruct
    outs = pl.pallas_call(
        functools.partial(step_kernel, n, blocks * width),
        out_shape=(
            shape((blocks, width), jnp.bfloat16),
            shape((own, width), jnp.float32),
            shape((own, width), jnp.bfloat16),
            shape((1, own), jnp.float32),
            shape((own, width), jnp.bfloat16),
            shape((1, own), jnp.float32),
        ),
        in_specs=[hbm] + [vmem] * 5,
        out_specs=[hbm] + [vmem] * 5,
        scratch_shapes=[
            pltpu.VMEM((blocks, width), jnp.bfloat16),
            pltpu.VMEM((n - 1, own, width), jnp.bfloat16),
            pltpu.VMEM((n, width), jnp.float32),
            pltpu.VMEM((own, width), jnp.bfloat16),
        ]
        + [pltpu.SemaphoreType.DMA] * 8,
        compiler_params=pltpu.CompilerParams(collective_id=0, has_side_effects=True),
    )(grads, master, first_q, first_scale.reshape(1, own), second_q, second_scale.reshape(1, own))
    weights, master_new, first_q_new, first_scale_new, second_q_new, second_scale_new = outs
    return (
        weights,
        master_new,
        first_q_new,
        first_scale_new.reshape(own),
        second_q_new,
        second_scale_new.reshape(own),
    )


def solution(mesh):
    placed = (P("dp", None, None), P("dp", None), P("dp", None), P("dp"), P("dp", None), P("dp"))
    return jax.shard_map(
        shards,
        mesh=mesh,
        in_specs=placed,
        out_specs=(P(), P("dp", None), P("dp", None), P("dp"), P("dp", None), P("dp")),
        check_vma=False,
    )
```

time: 109 us -> 27.4 us (0.25)
  blocking collectives: 80.8 us -> 0 us
  Pallas kernels: 0 us -> 22 us
  waiting for transfers between devices: 12.7 us -> 0 us
  starting transfers between devices: 8.24 us -> 0 us
  other arithmetic: 2.12 us -> 0 us
  local copies, waits for them, and re-layouts: 2.76 us -> 4.5 us
    all_gather x1 -> x0, blocking collectives: 40.8 us -> none  [shards(): lax.all_gather(master_new.astype(jnp.bfloat16), 'dp', axis=0, tiled=True)]
    psum x1 -> x0, blocking collectives: 40 us -> none  [shards(): squares = lax.psum(jnp.sum(total * total), 'dp')]
    pallas_call x0 -> x1, Pallas kernels: none -> 22 us  [shards(): pl.pallas_call(functools.partial(step_kernel, n, blocks * width), out_sha...]
    ppermute x5 -> x0, waiting for transfers between devices: 12.7 us -> none  [from_partner(): return lax.ppermute(block, axis, route)]
    ppermute x5 -> x0, starting transfers between devices: 8.24 us -> none  [from_partner(): return lax.ppermute(block, axis, route)]
    unnamed x17 -> x16, local copies, waits for them, and re-layouts: 1.82 us -> 4.5 us
  transfers between devices with their start and end apart: 5 -> 0, of which waited for: 5 -> 0; matrix products, arithmetic and copies ran while one was open for 0% -> 0% of each run, Pallas kernels for 0% -> 0%
where the time goes in v1:
time: 27.4 us; the launch traced here: 27.2 us
  Pallas kernels  22 us (80%)
  local copies, waits for them, and re-layouts  4.5 us (16%)
  between operations  0.66 us (2%)
    pallas_call x1, Pallas kernels, shards(): pl.pallas_call(functools.partial(step_kernel, n, blocks * width), out_sha...  22 us
    unnamed x16, local copies, waits for them, and re-layouts  4.5 us

profile of v1, /device:TPU:0, one launch (start us, length us, event | category | flops | bytes accessed | tf_op | source)
XLA Modules:
  0.0 27.2 jit_solution(14680463649620425784)
XLA Ops:
  0.6 22.0 %shard_map.109 = (bf16[512,128]{1,0:T(8,128)(2,1)}, f32[16,128]{1,0:T(8,128)}, bf16[16,128]{1,0:T(8,128)(2,1)}, f32[1,16]{1,0:T(1,128)}, bf16[16,128]{1,0:T(8,128)(2,1)}, /*index=5*/f32[1,16]{1,0:T(1,128)}) custom-call(bf16[1,512,128]{2,1,0:T(8,128)(2,1)} %grads_ref.1, f32[16,128]{1,0:T(8,128)} %master_ref.1, bf16[16,128]{1,0:T(8,128)(2,1)} %first_q_ref.1, ...), custom_call_target="tpu_custom_call" | custom-call | tf_op jit(solution)/shard_map/pallas_call | solution.py:170
  22.6 0.0 copy-start
  22.7 1.6 %copy.18 = bf16[512,128]{1,0:T(8,128)(2,1)} copy(bf16[512,128]{1,0:T(8,128)(2,1)} %get-tuple-element.24) | data formatting | bytes 262144
  24.2 0.0 copy-done
  24.2 0.0 copy-start.2
  24.2 0.6 %copy.19 = f32[16,128]{1,0:T(8,128)} copy(f32[16,128]{1,0:T(8,128)S(1)} %copy-done) | data formatting | bytes 16384
  24.8 0.1 copy-done.2
  24.9 0.0 copy-start.4
  24.9 0.0 copy-start.1
  24.9 0.6 %copy.20 = bf16[16,128]{1,0:T(8,128)(2,1)} copy(bf16[16,128]{1,0:T(8,128)(2,1)S(1)} %copy-done.2) | data formatting | bytes 8192
  25.5 0.0 copy-done.4
  25.5 0.5 %copy.21 = f32[16]{0:T(128)} copy(f32[16]{0:T(128)S(1)} %bitcast.7) | data formatting | bytes 128
  26.0 0.0 copy-done.1
  26.0 0.0 copy-start.3
  26.0 0.6 %copy.22 = bf16[16,128]{1,0:T(8,128)(2,1)} copy(bf16[16,128]{1,0:T(8,128)(2,1)S(1)} %copy-done.1) | data formatting | bytes 8192
  26.6 0.0 copy-done.3
  26.6 0.5 %copy.23 = f32[16]{0:T(128)} copy(f32[16]{0:T(128)S(1)} %bitcast.6) | data formatting | bytes 128
Async XLA Ops:
  22.6 1.6 %copy-start = (f32[16,128]{1,0:T(8,128)S(1)}, f32[16,128]{1,0:T(8,128)}, u32[]{:S(2)}) copy-start(f32[16,128]{1,0:T(8,128)} %get-tuple-element.25) | copy-start | bytes 24580
  24.2 0.7 %copy-start.2 = (bf16[16,128]{1,0:T(8,128)(2,1)S(1)}, bf16[16,128]{1,0:T(8,128)(2,1)}, u32[]{:S(2)}) copy-start(bf16[16,128]{1,0:T(8,128)(2,1)} %get-tuple-element.26) | copy-start | bytes 12292
  24.9 0.6 %copy-start.4 = (f32[1,16]{1,0:T(1,128)S(1)}, f32[1,16]{1,0:T(1,128)}, u32[]{:S(2)}) copy-start(f32[1,16]{1,0:T(1,128)} %get-tuple-element.15) | copy-start | bytes 196
  24.9 1.1 %copy-start.1 = (bf16[16,128]{1,0:T(8,128)(2,1)S(1)}, bf16[16,128]{1,0:T(8,128)(2,1)}, u32[]{:S(2)}) copy-start(bf16[16,128]{1,0:T(8,128)(2,1)} %get-tuple-element.28) | copy-start | bytes 12292
  26.0 0.6 %copy-start.3 = (f32[1,16]{1,0:T(1,128)S(1)}, f32[1,16]{1,0:T(1,128)}, u32[]{:S(2)}) copy-start(f32[1,16]{1,0:T(1,128)} %get-tuple-element.17) | copy-start | bytes 196

commit v2 on v1

v2 whole, which is shorter than its diff:
```python
import functools

import jax
import jax.numpy as jnp
from jax import lax
from jax.experimental import pallas as pl
from jax.experimental.pallas import tpu as pltpu
from jax.sharding import PartitionSpec as P

MESH = pl.DeviceIdType.MESH

beta_one = 0.9
beta_two = 0.95
learn_rate = 0.05
decay_rate = 0.1
adam_epsilon = 1e-08
clip_rms = 0.01
first_fix = 1.0 - 0.9**10
second_fix = 1.0 - 0.95**10


def column_of(row, count):
    down = lax.broadcasted_iota(jnp.int32, (count, count), 0)
    along = lax.broadcasted_iota(jnp.int32, (count, count), 1)
    spread = jnp.broadcast_to(row, (count, count))
    return jnp.sum(jnp.where(down == along, spread, 0.0), axis=1, keepdims=True)


def row_of(column, count):
    down = lax.broadcasted_iota(jnp.int32, (count, count), 0)
    along = lax.broadcasted_iota(jnp.int32, (count, count), 1)
    spread = jnp.broadcast_to(column, (count, count))
    return jnp.sum(jnp.where(down == along, spread, 0.0), axis=0, keepdims=True)


def step_kernel(
    n,
    entries,
    grads_ref,
    master_ref,
    first_q_ref,
    first_scale_ref,
    second_q_ref,
    second_scale_ref,
    weights_ref,
    master_new_ref,
    first_q_new_ref,
    first_scale_new_ref,
    second_q_new_ref,
    second_scale_new_ref,
    local,
    arrived,
    squares,
    mine,
    master,
    first_q,
    first_scale,
    second_q,
    second_scale,
    stage_sems,
    state_sems,
    grad_send,
    grad_recv,
    norm_send,
    norm_recv,
    gather_send,
    gather_recv,
):
    me = lax.axis_index("dp")
    own = master.shape[0]
    partners = [lax.rem(me + k, n) for k in range(1, n)]

    stage = pltpu.make_async_copy(grads_ref.at[0], local, stage_sems.at[0])
    stage.start()

    barrier = pltpu.get_barrier_semaphore()
    for to in partners:
        pl.semaphore_signal(barrier, inc=1, device_id=(to,), device_id_type=MESH)

    states = (
        (master_ref, master),
        (first_q_ref, first_q),
        (first_scale_ref, first_scale),
        (second_q_ref, second_q),
        (second_scale_ref, second_scale),
    )
    reads = [
        pltpu.make_async_copy(src, dst, state_sems.at[i]) for i, (src, dst) in enumerate(states)
    ]
    for read in reads:
        read.start()
    stage.wait()
    pl.semaphore_wait(barrier, n - 1)

    for k, to in enumerate(partners):
        pltpu.make_async_remote_copy(
            src_ref=local.at[pl.ds(pl.multiple_of(to * own, own), own)],
            dst_ref=arrived.at[k],
            send_sem=grad_send,
            recv_sem=grad_recv,
            device_id=(to,),
            device_id_type=MESH,
        ).start()

    for read in reads:
        read.wait()
    total = local[pl.ds(pl.multiple_of(me * own, own), own), :].astype(jnp.float32)
    first = beta_one * (first_q[...].astype(jnp.float32) * column_of(first_scale[...], own))
    second = beta_two * (second_q[...].astype(jnp.float32) * column_of(second_scale[...], own))
    kept = master[...] * (1.0 - learn_rate * decay_rate)
    pltpu.make_async_copy(arrived, arrived, grad_recv).wait()
    total = total + jnp.sum(arrived[...].astype(jnp.float32), axis=0)

    squares[pl.ds(n - 1, 1), :] = jnp.sum(total * total, axis=0, keepdims=True)
    for k, to in enumerate(partners):
        pltpu.make_async_remote_copy(
            src_ref=squares.at[pl.ds(n - 1, 1)],
            dst_ref=squares.at[pl.ds(k, 1)],
            send_sem=norm_send,
            recv_sem=norm_recv,
            device_id=(to,),
            device_id_type=MESH,
        ).start()

    others = squares.at[pl.ds(0, n - 1)]
    pltpu.make_async_copy(others, others, norm_recv).wait()
    norm = jnp.sqrt(jnp.sum(squares[...], keepdims=True))
    limit = clip_rms * jnp.sqrt(jnp.float32(entries))
    factor = jnp.minimum(1.0, limit / (norm + 1e-06))
    clipped = factor * total
    first_new = first + (1.0 - beta_one) * clipped
    second_new = second + (1.0 - beta_two) * clipped * clipped
    change = first_new / first_fix / (jnp.sqrt(second_new / second_fix) + adam_epsilon)
    master_new = kept - learn_rate * change
    mine[...] = master_new.astype(jnp.bfloat16)

    slot = weights_ref.at[pl.ds(pl.multiple_of(me * own, own), own)]
    for to in partners:
        pltpu.make_async_remote_copy(
            src_ref=mine,
            dst_ref=slot,
            send_sem=gather_send,
            recv_sem=gather_recv,
            device_id=(to,),
            device_id_type=MESH,
        ).start()
    keep = pltpu.make_async_copy(mine, slot, stage_sems.at[1])
    keep.start()

    first_top = jnp.max(jnp.abs(first_new), axis=1, keepdims=True) + 1e-08
    second_top = jnp.max(jnp.abs(second_new), axis=1, keepdims=True) + 1e-08
    master[...] = master_new
    first_q[...] = (first_new / first_top).astype(jnp.bfloat16)
    second_q[...] = (second_new / second_top).astype(jnp.bfloat16)
    first_scale[...] = row_of(first_top, own)
    second_scale[...] = row_of(second_top, own)
    results = (
        (master, master_new_ref),
        (first_q, first_q_new_ref),
        (first_scale, first_scale_new_ref),
        (second_q, second_q_new_ref),
        (second_scale, second_scale_new_ref),
    )
    writes = [
        pltpu.make_async_copy(src, dst, state_sems.at[i]) for i, (src, dst) in enumerate(results)
    ]
    for write in writes:
        write.start()

    sent = local.at[pl.ds(0, (n - 1) * own)]
    gathered = weights_ref.at[pl.ds(0, (n - 1) * own)]
    pltpu.make_async_copy(sent, sent, grad_send).wait()
    pltpu.make_async_copy(others, others, norm_send).wait()
    keep.wait()
    for write in writes:
        write.wait()
    pltpu.make_async_copy(sent, sent, gather_send).wait()
    pltpu.make_async_copy(gathered, gathered, gather_recv).wait()


def place_kernel(count, *refs):
    sems = refs[-1]
    copies = [
        pltpu.make_async_copy(refs[i], refs[count + i], sems.at[i]) for i in range(count)
    ]
    for copy in copies:
        copy.start()
    for copy in copies:
        copy.wait()


def shards(grads, master, first_q, first_scale, second_q, second_scale):
    n = lax.axis_size("dp")
    blocks, width = grads.shape[1:]
    own = master.shape[0]
    anywhere = pl.BlockSpec(memory_space=pl.ANY)
    shape = jax.ShapeDtypeStruct
    out_shape = (
        shape((blocks, width), jnp.bfloat16),
        shape((own, width), jnp.float32),
        shape((own, width), jnp.bfloat16),
        shape((1, own), jnp.float32),
        shape((own, width), jnp.bfloat16),
        shape((1, own), jnp.float32),
    )
    count = len(out_shape)
    outs = pl.pallas_call(
        functools.partial(step_kernel, n, blocks * width),
        out_shape=out_shape,
        in_specs=[anywhere] * 6,
        out_specs=[anywhere] * count,
        scratch_shapes=[
            pltpu.VMEM((blocks, width), jnp.bfloat16),
            pltpu.VMEM((n - 1, own, width), jnp.bfloat16),
            pltpu.VMEM((n, width), jnp.float32),
            pltpu.VMEM((own, width), jnp.bfloat16),
            pltpu.VMEM((own, width), jnp.float32),
            pltpu.VMEM((own, width), jnp.bfloat16),
            pltpu.VMEM((1, own), jnp.float32),
            pltpu.VMEM((own, width), jnp.bfloat16),
            pltpu.VMEM((1, own), jnp.float32),
            pltpu.SemaphoreType.DMA((2,)),
            pltpu.SemaphoreType.DMA((5,)),
        ]
        + [pltpu.SemaphoreType.DMA] * 6,
        compiler_params=pltpu.CompilerParams(collective_id=0, has_side_effects=True),
    )(grads, master, first_q, first_scale.reshape(1, own), second_q, second_scale.reshape(1, own))
    outs = pl.pallas_call(
        functools.partial(place_kernel, count),
        out_shape=out_shape,
        in_specs=[anywhere] * count,
        out_specs=[anywhere] * count,
        scratch_shapes=[pltpu.SemaphoreType.DMA((count,))],
    )(*outs)
    weights, master_new, first_q_new, first_scale_new, second_q_new, second_scale_new = outs
    return (
        weights,
        master_new,
        first_q_new,
        first_scale_new.reshape(own),
        second_q_new,
        second_scale_new.reshape(own),
    )


def solution(mesh):
    placed = (P("dp", None, None), P("dp", None), P("dp", None), P("dp"), P("dp", None), P("dp"))
    return jax.shard_map(
        shards,
        mesh=mesh,
        in_specs=placed,
        out_specs=(P(), P("dp", None), P("dp", None), P("dp"), P("dp", None), P("dp")),
        check_vma=False,
    )
```

time: 27.4 us -> 26.9 us (0.982)
  local copies, waits for them, and re-layouts: 4.5 us -> 0 us
  Pallas kernels: 22 us -> 26.1 us
    pallas_call x0 -> x1, Pallas kernels: none -> 5.66 us  [shards(): pl.pallas_call(functools.partial(place_kernel, count), out_shape=out_shap...]
    unnamed x16 -> x0, local copies, waits for them, and re-layouts: 4.5 us -> none
    pallas_call x1, Pallas kernels: 22 us -> 20.5 us  [shards(): pl.pallas_call(functools.partial(step_kernel, n, blocks * width), out_sha...]
where the time goes in v2:
time: 26.9 us; the launch traced here: 26.8 us
  Pallas kernels  26.1 us (97%)
  between operations  0.64 us (2%)
    pallas_call x1, Pallas kernels, shards(): pl.pallas_call(functools.partial(step_kernel, n, blocks * width), out_sha...  20.5 us
    pallas_call x1, Pallas kernels, shards(): pl.pallas_call(functools.partial(place_kernel, count), out_shape=out_shap...  5.66 us

profile of v2, /device:TPU:0, one launch (start us, length us, event | category | flops | bytes accessed | tf_op | source)
XLA Modules:
  0.0 26.8 jit_solution(509035302247257055)
XLA Ops:
  0.6 20.5 %shard_map.109 = (bf16[512,128]{1,0:T(8,128)(2,1)}, f32[16,128]{1,0:T(8,128)}, bf16[16,128]{1,0:T(8,128)(2,1)}, f32[1,16]{1,0:T(1,128)}, bf16[16,128]{1,0:T(8,128)(2,1)}, /*index=5*/f32[1,16]{1,0:T(1,128)}) custom-call(bf16[1,512,128]{2,1,0:T(8,128)(2,1)} %grads_ref.1, f32[16,128]{1,0:T(8,128)} %master_ref.1, bf16[16,128]{1,0:T(8,128)(2,1)} %first_q_ref.1, ...), custom_call_target="tpu_custom_call" | custom-call | tf_op jit(solution)/shard_map/pallas_call | solution.py:207
  21.1 5.7 %shard_map.110 = (bf16[512,128]{1,0:T(8,128)(2,1)}, f32[16,128]{1,0:T(8,128)}, bf16[16,128]{1,0:T(8,128)(2,1)}, f32[1,16]{1,0:T(1,128)}, bf16[16,128]{1,0:T(8,128)(2,1)}, /*index=5*/f32[1,16]{1,0:T(1,128)}) custom-call(bf16[512,128]{1,0:T(8,128)(2,1)} %get-tuple-element.18.refs_0_, f32[16,128]{1,0:T(8,128)} %get-tuple-element.19.refs_1_, ...), custom_call_target="tpu_custom_call" | custom-call | tf_op jit(solution)/shard_map/pallas_call | solution.py:228

commit v3 on v2

--- a/solution.py
+++ b/solution.py
@@ -149,31 +149,17 @@
 
     first_top = jnp.max(jnp.abs(first_new), axis=1, keepdims=True) + 1e-08
     second_top = jnp.max(jnp.abs(second_new), axis=1, keepdims=True) + 1e-08
-    master[...] = master_new
-    first_q[...] = (first_new / first_top).astype(jnp.bfloat16)
-    second_q[...] = (second_new / second_top).astype(jnp.bfloat16)
-    first_scale[...] = row_of(first_top, own)
-    second_scale[...] = row_of(second_top, own)
-    results = (
-        (master, master_new_ref),
-        (first_q, first_q_new_ref),
-        (first_scale, first_scale_new_ref),
-        (second_q, second_q_new_ref),
-        (second_scale, second_scale_new_ref),
-    )
-    writes = [
-        pltpu.make_async_copy(src, dst, state_sems.at[i]) for i, (src, dst) in enumerate(results)
-    ]
-    for write in writes:
-        write.start()
+    master_new_ref[...] = master_new
+    first_q_new_ref[...] = (first_new / first_top).astype(jnp.bfloat16)
+    second_q_new_ref[...] = (second_new / second_top).astype(jnp.bfloat16)
+    first_scale_new_ref[...] = row_of(first_top, own)
+    second_scale_new_ref[...] = row_of(second_top, own)
 
     sent = local.at[pl.ds(0, (n - 1) * own)]
     gathered = weights_ref.at[pl.ds(0, (n - 1) * own)]
     pltpu.make_async_copy(sent, sent, grad_send).wait()
     pltpu.make_async_copy(others, others, norm_send).wait()
     keep.wait()
-    for write in writes:
-        write.wait()
     pltpu.make_async_copy(sent, sent, gather_send).wait()
     pltpu.make_async_copy(gathered, gathered, gather_recv).wait()
 
@@ -194,6 +180,7 @@
     blocks, width = grads.shape[1:]
     own = master.shape[0]
     anywhere = pl.BlockSpec(memory_space=pl.ANY)
+    near = pl.BlockSpec(memory_space=pltpu.VMEM)
     shape = jax.ShapeDtypeStruct
     out_shape = (
         shape((blocks, width), jnp.bfloat16),
@@ -206,9 +193,9 @@
     count = len(out_shape)
     outs = pl.pallas_call(
         functools.partial(step_kernel, n, blocks * width),
-        out_shape=out_shape,
+        out_shape=tuple(pltpu.VMEM(out.shape, out.dtype) for out in out_shape),
         in_specs=[anywhere] * 6,
-        out_specs=[anywhere] * count,
+        out_specs=[near] * count,
         scratch_shapes=[
             pltpu.VMEM((blocks, width), jnp.bfloat16),
             pltpu.VMEM((n - 1, own, width), jnp.bfloat16),
@@ -228,7 +215,7 @@
     outs = pl.pallas_call(
         functools.partial(place_kernel, count),
         out_shape=out_shape,
-        in_specs=[anywhere] * count,
+        in_specs=[near] * count,
         out_specs=[anywhere] * count,
         scratch_shapes=[pltpu.SemaphoreType.DMA((count,))],
     )(*outs)

time: 26.9 us -> 26.2 us (0.974)
  Pallas kernels: 26.1 us -> 21.8 us
  local copies, waits for them, and re-layouts: 0 us -> 3.6 us
    pallas_call x1, Pallas kernels: 5.66 us -> 1.65 us  [shards(): pl.pallas_call(functools.partial(place_kernel, count), out_shape=out_shap...]
    unnamed x0 -> x12, local copies, waits for them, and re-layouts: none -> 3.6 us
    pallas_call x1, Pallas kernels: 20.5 us -> 20.2 us  [shards(): pl.pallas_call(functools.partial(step_kernel, n, blocks * width), out_sha...]
where the time goes in v3:
time: 26.2 us; the launch traced here: 26.1 us
  Pallas kernels  21.8 us (83%)
  local copies, waits for them, and re-layouts  3.6 us (14%)
  between operations  0.66 us (3%)
    pallas_call x1, Pallas kernels, shards(): pl.pallas_call(functools.partial(step_kernel, n, blocks * width), out_sha...  20.2 us
    unnamed x12, local copies, waits for them, and re-layouts  3.6 us
    pallas_call x1, Pallas kernels, shards(): pl.pallas_call(functools.partial(place_kernel, count), out_shape=out_shap...  1.65 us

profile of v3, /device:TPU:0, one launch (start us, length us, event | category | flops | bytes accessed | tf_op | source)
XLA Modules:
  0.0 26.1 jit_solution(10165816242488004299)
XLA Ops:
  0.6 20.2 %shard_map.109 = (bf16[512,128]{1,0:T(8,128)(2,1)S(1)}, f32[16,128]{1,0:T(8,128)S(1)}, bf16[16,128]{1,0:T(8,128)(2,1)S(1)}, f32[1,16]{1,0:T(1,128)S(1)}, bf16[16...) custom-call(bf16[1,512,128]{2,1,0:T(8,128)(2,1)} %grads_ref.1, f32[16,128]{1,0:T(8,128)} %master_ref.1, ...), custom_call_target="tpu_custom_call" | custom-call | tf_op jit(solution)/shard_map/pallas_call | solution.py:194
  20.8 0.0 copy-start
  20.8 0.6 %copy-done = bf16[512,128]{1,0:T(8,128)(2,1)} copy-done((bf16[512,128]{1,0:T(8,128)(2,1)}, bf16[512,128]{1,0:T(8,128)(2,1)S(1)}, u32[]{:S(2)}) %copy-start) | copy-done | bytes 131096
  21.4 0.0 copy-start.2
  21.5 0.6 %copy-done.2 = bf16[16,128]{1,0:T(8,128)(2,1)} copy-done((bf16[16,128]{1,0:T(8,128)(2,1)}, bf16[16,128]{1,0:T(8,128)(2,1)S(1)}, u32[]{:S(2)}) %copy-start.2) | copy-done | bytes 4120
  22.0 0.0 copy-start.3
  22.0 0.6 %copy-done.3 = bf16[16,128]{1,0:T(8,128)(2,1)} copy-done((bf16[16,128]{1,0:T(8,128)(2,1)}, bf16[16,128]{1,0:T(8,128)(2,1)S(1)}, u32[]{:S(2)}) %copy-start.3) | copy-done | bytes 4120
  22.6 0.0 copy-start.4
  22.6 0.6 %copy-done.4 = f32[1,16]{1,0:T(1,128)} copy-done((f32[1,16]{1,0:T(1,128)}, f32[1,16]{1,0:T(1,128)S(1)}, u32[]{:S(2)}) %copy-start.4) | copy-done | bytes 88
  23.2 0.0 copy-start.5
  23.2 0.6 %copy-done.5 = f32[1,16]{1,0:T(1,128)} copy-done((f32[1,16]{1,0:T(1,128)}, f32[1,16]{1,0:T(1,128)S(1)}, u32[]{:S(2)}) %copy-start.5) | copy-done | bytes 88
  23.8 0.0 copy-start.1
  23.8 0.6 %copy-done.1 = f32[16,128]{1,0:T(8,128)} copy-done((f32[16,128]{1,0:T(8,128)}, f32[16,128]{1,0:T(8,128)S(1)}, u32[]{:S(2)}) %copy-start.1) | copy-done | bytes 8216
  24.4 1.6 %shard_map.110 = (bf16[512,128]{1,0:T(8,128)(2,1)}, f32[16,128]{1,0:T(8,128)}, bf16[16,128]{1,0:T(8,128)(2,1)}, f32[1,16]{1,0:T(1,128)}, bf16[16,128]{1,0:T(8,128)(2,1)}, /*index=5*/f32[1,16]{1,0:T(1,128)}) custom-call(bf16[512,128]{1,0:T(8,128)(2,1)} %copy-done, f32[16,128]{1,0:T(8,128)} %copy-done.1, bf16[16,128]{1,0:T(8,128)(2,1)} %copy-done.2, ...), custom_call_target="tpu_custom_call" | custom-call | tf_op jit(solution)/shard_map/pallas_call | solution.py:215
Async XLA Ops:
  20.8 0.7 %copy-start = (bf16[512,128]{1,0:T(8,128)(2,1)}, bf16[512,128]{1,0:T(8,128)(2,1)S(1)}, u32[]{:S(2)}) copy-start(bf16[512,128]{1,0:T(8,128)(2,1)S(1)} %get-tuple-element.18.refs_0_) | copy-start | bytes 393220
  21.4 0.6 %copy-start.2 = (bf16[16,128]{1,0:T(8,128)(2,1)}, bf16[16,128]{1,0:T(8,128)(2,1)S(1)}, u32[]{:S(2)}) copy-start(bf16[16,128]{1,0:T(8,128)(2,1)S(1)} %get-tuple-element.20.refs_2_) | copy-start | bytes 12292
  22.0 0.6 %copy-start.3 = (bf16[16,128]{1,0:T(8,128)(2,1)}, bf16[16,128]{1,0:T(8,128)(2,1)S(1)}, u32[]{:S(2)}) copy-start(bf16[16,128]{1,0:T(8,128)(2,1)S(1)} %get-tuple-element.22.refs_4_) | copy-start | bytes 12292
  22.6 0.6 %copy-start.4 = (f32[1,16]{1,0:T(1,128)}, f32[1,16]{1,0:T(1,128)S(1)}, u32[]{:S(2)}) copy-start(f32[1,16]{1,0:T(1,128)S(1)} %get-tuple-element.21.refs_3_) | copy-start | bytes 196
  23.2 0.6 %copy-start.5 = (f32[1,16]{1,0:T(1,128)}, f32[1,16]{1,0:T(1,128)S(1)}, u32[]{:S(2)}) copy-start(f32[1,16]{1,0:T(1,128)S(1)} %get-tuple-element.23.refs_5_) | copy-start | bytes 196
  23.8 0.6 %copy-start.1 = (f32[16,128]{1,0:T(8,128)}, f32[16,128]{1,0:T(8,128)S(1)}, u32[]{:S(2)}) copy-start(f32[16,128]{1,0:T(8,128)S(1)} %get-tuple-element.19.refs_1_) | copy-start | bytes 24580

commit v4 on v3

--- a/solution.py
+++ b/solution.py
@@ -218,7 +218,7 @@
         in_specs=[near] * count,
         out_specs=[anywhere] * count,
         scratch_shapes=[pltpu.SemaphoreType.DMA((count,))],
-    )(*outs)
+    )(*[pltpu.with_memory_space_constraint(out, pltpu.VMEM) for out in outs])
     weights, master_new, first_q_new, first_scale_new, second_q_new, second_scale_new = outs
     return (
         weights,

time: 26.2 us -> 21.7 us (0.83)
  local copies, waits for them, and re-layouts: 3.6 us -> 0 us
  Pallas kernels: 21.8 us -> 20.9 us
    unnamed x12 -> x0, local copies, waits for them, and re-layouts: 3.6 us -> none
    pallas_call x1, Pallas kernels: 1.65 us -> 0.72 us  [shards(): pl.pallas_call(functools.partial(place_kernel, count), out_shape=out_shap...]
where the time goes in v4:
time: 21.7 us; the launch traced here: 21.5 us
  Pallas kernels  20.9 us (96%)
  between operations  0.64 us (3%)
    pallas_call x1, Pallas kernels, shards(): pl.pallas_call(functools.partial(step_kernel, n, blocks * width), out_sha...  20.2 us
    pallas_call x1, Pallas kernels, shards(): pl.pallas_call(functools.partial(place_kernel, count), out_shape=out_shap...  0.72 us

profile of v4, /device:TPU:0, one launch (start us, length us, event | category | flops | bytes accessed | tf_op | source)
XLA Modules:
  0.0 21.5 jit_solution(3308634699241163185)
XLA Ops:
  0.6 20.2 %shard_map.109 = (bf16[512,128]{1,0:T(8,128)(2,1)S(1)}, f32[16,128]{1,0:T(8,128)S(1)}, bf16[16,128]{1,0:T(8,128)(2,1)S(1)}, f32[1,16]{1,0:T(1,128)S(1)}, bf16[16...) custom-call(bf16[1,512,128]{2,1,0:T(8,128)(2,1)} %grads_ref.1, f32[16,128]{1,0:T(8,128)} %master_ref.1, ...), custom_call_target="tpu_custom_call" | custom-call | tf_op jit(solution)/shard_map/pallas_call | solution.py:194
  20.8 0.7 %shard_map.110 = (bf16[512,128]{1,0:T(8,128)(2,1)}, f32[16,128]{1,0:T(8,128)}, bf16[16,128]{1,0:T(8,128)(2,1)}, f32[1,16]{1,0:T(1,128)}, bf16[16,128]{1,0:T(8,128)(2,1)}, /*index=5*/f32[1,16]{1,0:T(1,128)}) custom-call(bf16[512,128]{1,0:T(8,128)(2,1)S(1)} %get-tuple-element.18.refs_0_, f32[16,128]{1,0:T(8,128)S(1)} %get-tuple-element.19.refs_1_, ...), custom_call_target="tpu_custom_call" | custom-call | tf_op jit(solution)/shard_map/pallas_call | solution.py:215

commit v5 on v4

v5 whole, which is shorter than its diff:
```python
import functools

import jax
import jax.numpy as jnp
from jax import lax
from jax.experimental import pallas as pl
from jax.experimental.pallas import tpu as pltpu
from jax.sharding import PartitionSpec as P

MESH = pl.DeviceIdType.MESH

beta_one = 0.9
beta_two = 0.95
learn_rate = 0.05
decay_rate = 0.1
adam_epsilon = 1e-08
clip_rms = 0.01
first_fix = 1.0 - 0.9**10
second_fix = 1.0 - 0.95**10


def column_of(row, count):
    down = lax.broadcasted_iota(jnp.int32, (count, count), 0)
    along = lax.broadcasted_iota(jnp.int32, (count, count), 1)
    spread = jnp.broadcast_to(row, (count, count))
    return jnp.sum(jnp.where(down == along, spread, 0.0), axis=1, keepdims=True)


def row_of(column, count):
    down = lax.broadcasted_iota(jnp.int32, (count, count), 0)
    along = lax.broadcasted_iota(jnp.int32, (count, count), 1)
    spread = jnp.broadcast_to(column, (count, count))
    return jnp.sum(jnp.where(down == along, spread, 0.0), axis=0, keepdims=True)


def push(src, dst, send_sem, recv_sem, to):
    pltpu.make_async_remote_copy(
        src_ref=src,
        dst_ref=dst,
        send_sem=send_sem,
        recv_sem=recv_sem,
        device_id=(to,),
        device_id_type=MESH,
    ).start()


def drain(ref, sem):
    pltpu.make_async_copy(ref, ref, sem).wait()


def step_kernel(
    outer,
    inner,
    entries,
    grads_ref,
    master_ref,
    first_q_ref,
    first_scale_ref,
    second_q_ref,
    second_scale_ref,
    weights_ref,
    master_new_ref,
    first_q_new_ref,
    first_scale_new_ref,
    second_q_new_ref,
    second_scale_new_ref,
    local,
    near_grads,
    partial,
    far_grads,
    near_squares,
    far_squares,
    master,
    first_q,
    first_scale,
    second_q,
    second_scale,
    stage_sem,
    state_sems,
    send_sems,
    recv_sems,
):
    me = lax.axis_index("dp")
    own = master.shape[0]
    group = lax.div(me, inner)
    place = lax.rem(me, inner)
    near_places = [lax.rem(place + k, inner) for k in range(1, inner)]
    near = [group * inner + p for p in near_places]
    far_groups = [lax.rem(group + k, outer) for k in range(1, outer)]
    far = [g * inner + place for g in far_groups]

    stage = pltpu.make_async_copy(grads_ref, local, stage_sem)
    stage.start()
    barrier = pltpu.get_barrier_semaphore()
    for to in near + far:
        pl.semaphore_signal(barrier, inc=1, device_id=(to,), device_id_type=MESH)

    states = (
        (master_ref, master),
        (first_q_ref, first_q),
        (first_scale_ref, first_scale),
        (second_q_ref, second_q),
        (second_scale_ref, second_scale),
    )
    reads = [
        pltpu.make_async_copy(src, dst, state_sems.at[i]) for i, (src, dst) in enumerate(states)
    ]
    for read in reads:
        read.start()
    stage.wait()
    pl.semaphore_wait(barrier, inner + outer - 2)

    for k, (p, to) in enumerate(zip(near_places, near)):
        push(local.at[:, p], near_grads.at[k], send_sems.at[0], recv_sems.at[0], to)
    for read in reads:
        read.wait()
    first = beta_one * (first_q[...].astype(jnp.float32) * column_of(first_scale[...], own))
    second = beta_two * (second_q[...].astype(jnp.float32) * column_of(second_scale[...], own))
    kept = master[...] * (1.0 - learn_rate * decay_rate)
    drain(near_grads, recv_sems.at[0])
    sums = local[:, place].astype(jnp.float32)
    partial[...] = sums + jnp.sum(near_grads[...].astype(jnp.float32), axis=0)

    for k, (g, to) in enumerate(zip(far_groups, far)):
        push(partial.at[g], far_grads.at[k], send_sems.at[1], recv_sems.at[1], to)
    drain(far_grads, recv_sems.at[1])
    total = partial[group] + jnp.sum(far_grads[...], axis=0)

    far_squares[pl.ds(outer - 1, 1), :] = jnp.sum(total * total, axis=0, keepdims=True)
    for k, to in enumerate(far):
        push(
            far_squares.at[pl.ds(outer - 1, 1)],
            far_squares.at[pl.ds(k, 1)],
            send_sems.at[2],
            recv_sems.at[2],
            to,
        )
    far_rows = far_squares.at[pl.ds(0, outer - 1)]
    drain(far_rows, recv_sems.at[2])
    near_squares[pl.ds(inner - 1, 1), :] = jnp.sum(far_squares[...], axis=0, keepdims=True)
    for k, to in enumerate(near):
        push(
            near_squares.at[pl.ds(inner - 1, 1)],
            near_squares.at[pl.ds(k, 1)],
            send_sems.at[3],
            recv_sems.at[3],
            to,
        )
    near_rows = near_squares.at[pl.ds(0, inner - 1)]
    drain(near_rows, recv_sems.at[3])
    norm = jnp.sqrt(jnp.sum(near_squares[...], keepdims=True))
    limit = clip_rms * jnp.sqrt(jnp.float32(entries))
    factor = jnp.minimum(1.0, limit / (norm + 1e-06))
    clipped = factor * total
    first_new = first + (1.0 - beta_one) * clipped
    second_new = second + (1.0 - beta_two) * clipped * clipped
    change = first_new / first_fix / (jnp.sqrt(second_new / second_fix) + adam_epsilon)
    master_new = kept - learn_rate * change
    weights_ref[group, place] = master_new.astype(jnp.bfloat16)

    slot = weights_ref.at[group, place]
    for to in far:
        push(slot, slot, send_sems.at[4], recv_sems.at[4], to)

    first_top = jnp.max(jnp.abs(first_new), axis=1, keepdims=True) + 1e-08
    second_top = jnp.max(jnp.abs(second_new), axis=1, keepdims=True) + 1e-08
    master_new_ref[...] = master_new
    first_q_new_ref[...] = (first_new / first_top).astype(jnp.bfloat16)
    second_q_new_ref[...] = (second_new / second_top).astype(jnp.bfloat16)
    first_scale_new_ref[...] = row_of(first_top, own)
    second_scale_new_ref[...] = row_of(second_top, own)

    far_weights = weights_ref.at[pl.ds(0, outer - 1), 0]
    drain(far_weights, recv_sems.at[4])
    column = weights_ref.at[:, place]
    for to in near:
        push(column, column, send_sems.at[5], recv_sems.at[5], to)

    drain(near_grads, send_sems.at[0])
    drain(far_grads, send_sems.at[1])
    drain(far_rows, send_sems.at[2])
    drain(near_rows, send_sems.at[3])
    drain(far_weights, send_sems.at[4])
    near_weights = weights_ref.at[:, pl.ds(0, inner - 1)]
    drain(near_weights, send_sems.at[5])
    drain(near_weights, recv_sems.at[5])


def place_kernel(count, *refs):
    sems = refs[-1]
    copies = [
        pltpu.make_async_copy(refs[i], refs[count + i], sems.at[i]) for i in range(count)
    ]
    for copy in copies:
        copy.start()
    for copy in copies:
        copy.wait()


def shards(grads, master, first_q, first_scale, second_q, second_scale):
    n = lax.axis_size("dp")
    blocks, width = grads.shape[1:]
    own = master.shape[0]
    inner = 1
    while inner * inner < n:
        inner *= 2
    outer = n // inner
    anywhere = pl.BlockSpec(memory_space=pl.ANY)
    near = pl.BlockSpec(memory_space=pltpu.VMEM)
    shape = jax.ShapeDtypeStruct
    out_shape = (
        shape((outer, inner, own, width), jnp.bfloat16),
        shape((own, width), jnp.float32),
        shape((own, width), jnp.bfloat16),
        shape((1, own), jnp.float32),
        shape((own, width), jnp.bfloat16),
        shape((1, own), jnp.float32),
    )
    count = len(out_shape)
    outs = pl.pallas_call(
        functools.partial(step_kernel, outer, inner, blocks * width),
        out_shape=tuple(pltpu.VMEM(out.shape, out.dtype) for out in out_shape),
        in_specs=[anywhere] * 6,
        out_specs=[near] * count,
        scratch_shapes=[
            pltpu.VMEM((outer, inner, own, width), jnp.bfloat16),
            pltpu.VMEM((inner - 1, outer, own, width), jnp.bfloat16),
            pltpu.VMEM((outer, own, width), jnp.float32),
            pltpu.VMEM((outer - 1, own, width), jnp.float32),
            pltpu.VMEM((inner, width), jnp.float32),
            pltpu.VMEM((outer, width), jnp.float32),
            pltpu.VMEM((own, width), jnp.float32),
            pltpu.VMEM((own, width), jnp.bfloat16),
            pltpu.VMEM((1, own), jnp.float32),
            pltpu.VMEM((own, width), jnp.bfloat16),
            pltpu.VMEM((1, own), jnp.float32),
            pltpu.SemaphoreType.DMA,
            pltpu.SemaphoreType.DMA((5,)),
            pltpu.SemaphoreType.DMA((6,)),
            pltpu.SemaphoreType.DMA((6,)),
        ],
        compiler_params=pltpu.CompilerParams(collective_id=0, has_side_effects=True),
    )(grads.reshape(outer, inner, own, width), master, first_q, first_scale.reshape(1, own), second_q, second_scale.reshape(1, own))
    outs = pl.pallas_call(
        functools.partial(place_kernel, count),
        out_shape=out_shape,
        in_specs=[near] * count,
        out_specs=[anywhere] * count,
        scratch_shapes=[pltpu.SemaphoreType.DMA((count,))],
    )(*[pltpu.with_memory_space_constraint(out, pltpu.VMEM) for out in outs])
    weights, master_new, first_q_new, first_scale_new, second_q_new, second_scale_new = outs
    return (
        weights.reshape(blocks, width),
        master_new,
        first_q_new,
        first_scale_new.reshape(own),
        second_q_new,
        second_scale_new.reshape(own),
    )


def solution(mesh):
    placed = (P("dp", None, None), P("dp", None), P("dp", None), P("dp"), P("dp", None), P("dp"))
    return jax.shard_map(
        shards,
        mesh=mesh,
        in_specs=placed,
        out_specs=(P(), P("dp", None), P("dp", None), P("dp"), P("dp", None), P("dp")),
        check_vma=False,
    )
```

time: 21.7 us -> 27.3 us (1.26)
  Pallas kernels: 20.9 us -> 26.5 us
    pallas_call x1, Pallas kernels: 20.2 us -> 25.8 us  [shards(): pl.pallas_call(functools.partial(step_kernel, outer, inner, blocks * widt...]
where the time goes in v5:
time: 27.3 us; the launch traced here: 27.1 us
  Pallas kernels  26.5 us (97%)
  between operations  0.64 us (2%)
    pallas_call x1, Pallas kernels, shards(): pl.pallas_call(functools.partial(step_kernel, outer, inner, blocks * widt...  25.8 us
    pallas_call x1, Pallas kernels, shards(): pl.pallas_call(functools.partial(place_kernel, count), out_shape=out_shap...  0.72 us

profile of v5, /device:TPU:0, one launch (start us, length us, event | category | flops | bytes accessed | tf_op | source)
XLA Modules:
  0.0 27.1 jit_solution(1834493079611814270)
XLA Ops:
  0.6 25.8 %shard_map.109 = (bf16[4,8,16,128]{3,2,1,0:T(8,128)(2,1)S(1)}, f32[16,128]{1,0:T(8,128)S(1)}, bf16[16,128]{1,0:T(8,128)(2,1)S(1)}, f32[1,16]{1,0:T(1,128)S(1)}, ...) custom-call(bf16[4,8,16,128]{3,2,1,0:T(8,128)(2,1)} %bitcast.6, f32[16,128]{1,0:T(8,128)} %master_ref.1, ...), custom_call_target="tpu_custom_call" | custom-call | tf_op jit(solution)/shard_map/pallas_call | solution.py:220
  26.4 0.7 %shard_map.110 = (bf16[4,8,16,128]{3,2,1,0:T(8,128)(2,1)}, f32[16,128]{1,0:T(8,128)}, bf16[16,128]{1,0:T(8,128)(2,1)}, f32[1,16]{1,0:T(1,128)}, bf16[16,128]{1,0:T(8,128)(2,1)}, /*index=5*/f32[1,16]{1,0:T(1,128)}) custom-call(bf16[4,8,16,128]{3,2,1,0:T(8,128)(2,1)S(1)} %get-tuple-element.18.refs_0_, f32[16,128]{1,0:T(8,128)S(1)} %get-tuple-element.19.refs_1_, ...), custom_call_target="tpu_custom_call" | custom-call | tf_op jit(solution)/shard_map/pallas_call | solution.py:244

commit v6 on v4

--- a/solution.py
+++ b/solution.py
@@ -68,13 +68,14 @@
 ):
     me = lax.axis_index("dp")
     own = master.shape[0]
-    partners = [lax.rem(me + k, n) for k in range(1, n)]
+    order = sorted(range(1, n), key=lambda k: abs(2 * k - n))
+    partners = [(k - 1, lax.rem(me + k, n)) for k in order]
 
     stage = pltpu.make_async_copy(grads_ref.at[0], local, stage_sems.at[0])
     stage.start()
 
     barrier = pltpu.get_barrier_semaphore()
-    for to in partners:
+    for _, to in partners:
         pl.semaphore_signal(barrier, inc=1, device_id=(to,), device_id_type=MESH)
 
     states = (
@@ -92,7 +93,7 @@
     stage.wait()
     pl.semaphore_wait(barrier, n - 1)
 
-    for k, to in enumerate(partners):
+    for k, to in partners:
         pltpu.make_async_remote_copy(
             src_ref=local.at[pl.ds(pl.multiple_of(to * own, own), own)],
             dst_ref=arrived.at[k],
@@ -112,7 +113,7 @@
     total = total + jnp.sum(arrived[...].astype(jnp.float32), axis=0)
 
     squares[pl.ds(n - 1, 1), :] = jnp.sum(total * total, axis=0, keepdims=True)
-    for k, to in enumerate(partners):
+    for k, to in partners:
         pltpu.make_async_remote_copy(
             src_ref=squares.at[pl.ds(n - 1, 1)],
             dst_ref=squares.at[pl.ds(k, 1)],
@@ -135,7 +136,7 @@
     mine[...] = master_new.astype(jnp.bfloat16)
 
     slot = weights_ref.at[pl.ds(pl.multiple_of(me * own, own), own)]
-    for to in partners:
+    for _, to in partners:
         pltpu.make_async_remote_copy(
             src_ref=mine,
             dst_ref=slot,

time: 21.7 us -> 23.1 us (1.065)
  Pallas kernels: 20.9 us -> 22.3 us
    pallas_call x1, Pallas kernels: 20.2 us -> 21.6 us  [shards(): pl.pallas_call(functools.partial(step_kernel, n, blocks * width), out_sha...]
where the time goes in v6:
time: 23.1 us; the launch traced here: 23 us
  Pallas kernels  22.3 us (97%)
  between operations  0.64 us (3%)
    pallas_call x1, Pallas kernels, shards(): pl.pallas_call(functools.partial(step_kernel, n, blocks * width), out_sha...  21.6 us
    pallas_call x1, Pallas kernels, shards(): pl.pallas_call(functools.partial(place_kernel, count), out_shape=out_shap...  0.72 us

profile of v6, /device:TPU:0, one launch (start us, length us, event | category | flops | bytes accessed | tf_op | source)
XLA Modules:
  0.0 23.0 jit_solution(1250457662057944467)
XLA Ops:
  0.6 21.6 %shard_map.109 = (bf16[512,128]{1,0:T(8,128)(2,1)S(1)}, f32[16,128]{1,0:T(8,128)S(1)}, bf16[16,128]{1,0:T(8,128)(2,1)S(1)}, f32[1,16]{1,0:T(1,128)S(1)}, bf16[16...) custom-call(bf16[1,512,128]{2,1,0:T(8,128)(2,1)} %grads_ref.1, f32[16,128]{1,0:T(8,128)} %master_ref.1, ...), custom_call_target="tpu_custom_call" | custom-call | tf_op jit(solution)/shard_map/pallas_call | solution.py:195
  22.3 0.7 %shard_map.110 = (bf16[512,128]{1,0:T(8,128)(2,1)}, f32[16,128]{1,0:T(8,128)}, bf16[16,128]{1,0:T(8,128)(2,1)}, f32[1,16]{1,0:T(1,128)}, bf16[16,128]{1,0:T(8,128)(2,1)}, /*index=5*/f32[1,16]{1,0:T(1,128)}) custom-call(bf16[512,128]{1,0:T(8,128)(2,1)S(1)} %get-tuple-element.18.refs_0_, f32[16,128]{1,0:T(8,128)S(1)} %get-tuple-element.19.refs_1_, ...), custom_call_target="tpu_custom_call" | custom-call | tf_op jit(solution)/shard_map/pallas_call | solution.py:216

commit v7 on v6

--- a/solution.py
+++ b/solution.py
@@ -68,7 +68,7 @@
 ):
     me = lax.axis_index("dp")
     own = master.shape[0]
-    order = sorted(range(1, n), key=lambda k: abs(2 * k - n))
+    order = sorted(range(1, n), key=lambda k: -abs(2 * k - n))
     partners = [(k - 1, lax.rem(me + k, n)) for k in order]
 
     stage = pltpu.make_async_copy(grads_ref.at[0], local, stage_sems.at[0])

time: 23.1 us -> 22.4 us (0.970)
  Pallas kernels: 22.3 us -> 21.6 us
    pallas_call x1, Pallas kernels: 21.6 us -> 20.9 us  [shards(): pl.pallas_call(functools.partial(step_kernel, n, blocks * width), out_sha...]
where the time goes in v7:
time: 22.4 us; the launch traced here: 22.2 us
  Pallas kernels  21.6 us (96%)
  between operations  0.64 us (3%)
    pallas_call x1, Pallas kernels, shards(): pl.pallas_call(functools.partial(step_kernel, n, blocks * width), out_sha...  20.9 us
    pallas_call x1, Pallas kernels, shards(): pl.pallas_call(functools.partial(place_kernel, count), out_shape=out_shap...  0.72 us

profile of v7, /device:TPU:0, one launch (start us, length us, event | category | flops | bytes accessed | tf_op | source)
XLA Modules:
  0.0 22.2 jit_solution(16010871624364416322)
XLA Ops:
  0.6 20.9 %shard_map.109 = (bf16[512,128]{1,0:T(8,128)(2,1)S(1)}, f32[16,128]{1,0:T(8,128)S(1)}, bf16[16,128]{1,0:T(8,128)(2,1)S(1)}, f32[1,16]{1,0:T(1,128)S(1)}, bf16[16...) custom-call(bf16[1,512,128]{2,1,0:T(8,128)(2,1)} %grads_ref.1, f32[16,128]{1,0:T(8,128)} %master_ref.1, ...), custom_call_target="tpu_custom_call" | custom-call | tf_op jit(solution)/shard_map/pallas_call | solution.py:195
  21.5 0.7 %shard_map.110 = (bf16[512,128]{1,0:T(8,128)(2,1)}, f32[16,128]{1,0:T(8,128)}, bf16[16,128]{1,0:T(8,128)(2,1)}, f32[1,16]{1,0:T(1,128)}, bf16[16,128]{1,0:T(8,128)(2,1)}, /*index=5*/f32[1,16]{1,0:T(1,128)}) custom-call(bf16[512,128]{1,0:T(8,128)(2,1)S(1)} %get-tuple-element.18.refs_0_, f32[16,128]{1,0:T(8,128)S(1)} %get-tuple-element.19.refs_1_, ...), custom_call_target="tpu_custom_call" | custom-call | tf_op jit(solution)/shard_map/pallas_call | solution.py:216
